TPU v7x, 32 devices: a whole 2x2x4 slice. The times are simulated.
32 devices in a mesh: batch: 8 (over z, x), seq: 4 (over y, core).
Axes of the slice: x: 2, y: 2, z: 4, core: 2. Of those that a mesh axis runs over, the one named last changes fastest.
Arguments:
- hidden_in: bfloat16 [24, 512, 768], P('batch', 'seq'), may hold values from -6 to 6
- cotangent: bfloat16 [24, 512, 768], P('batch', 'seq'), may hold values from -6 to 6
- span_mask: int32 [24, 512], P('batch', 'seq'), may hold values from 0 to 1, as said below
- lengths: int32 [24], P('batch'), may hold values from 128 to 512, as said below
- repeats: int32 [24], P('batch'), may hold values from 1 to 4
- mask_embedding: bfloat16 [768], replicated, may hold values from -6 to 6
- query_weight: bfloat16 [768, 768], replicated, may hold values from -0.21875 to 0.21875
- query_bias: bfloat16 [768], replicated, may hold values from -2 to 2
- key_weight: bfloat16 [768, 768], replicated, may hold values from -0.21875 to 0.21875
- value_weight: bfloat16 [768, 768], replicated, may hold values from -0.21875 to 0.21875
- value_bias: bfloat16 [768], replicated, may hold values from -2 to 2
- output_weight: bfloat16 [768, 768], replicated, may hold values from -2.5 to 2.5
- output_bias: bfloat16 [768], replicated, may hold values from -2 to 2
- mixing_gain: bfloat16 [768], replicated, may hold values from 0.25 to 1.75
- mixing_shift: bfloat16 [768], replicated, may hold values from -2 to 2
- inner_weight: bfloat16 [768, 3072], replicated, may hold values from -0.21875 to 0.21875
- inner_bias: bfloat16 [3072], replicated, may hold values from -2 to 2
- outer_weight: bfloat16 [3072, 768], replicated, may hold values from -0.21875 to 0.21875
- outer_bias: bfloat16 [768], replicated, may hold values from -2 to 2
- final_gain: bfloat16 [768], replicated, may hold values from 0.25 to 1.75
- final_shift: bfloat16 [768], replicated, may hold values from -2 to 2
Outputs:
- layer_out: bfloat16 [24, 512, 768], P('batch', 'seq')
- grad_input: bfloat16 [24, 512, 768], P('batch', 'seq')
- gradient_mask_embedding: float32 [768], replicated
- gradient_query_weight: float32 [768, 768], P('batch', 'seq')
- gradient_query_bias: float32 [768], replicated
- gradient_key_weight: float32 [768, 768], P('batch', 'seq')
- gradient_value_weight: float32 [768, 768], P('batch', 'seq')
- gradient_value_bias: float32 [768], replicated
- gradient_output_weight: float32 [768, 768], P('batch', 'seq')
- gradient_output_bias: float32 [768], replicated
- gradient_mixing_gain: float32 [768], replicated
- gradient_mixing_shift: float32 [768], replicated
- gradient_inner_weight: float32 [768, 3072], P('batch', 'seq')
- gradient_inner_bias: float32 [3072], replicated
- gradient_outer_weight: float32 [3072, 768], P('batch', 'seq')
- gradient_outer_bias: float32 [768], replicated
- gradient_final_gain: float32 [768], replicated
- gradient_final_shift: float32 [768], replicated
Inputs may be any that keep to these rules, and one draw needn't show every extreme that they name: `lengths`: in every aligned block of 3 rows, at least one row has length 512. `span_mask`: A union of runs of 6 positions; each row has a run that ends or starts within two positions of a multiple of 128 without crossing it.
All inputs are finite; a program needn't handle non-finite values.
Results may differ from a plain program's by a relative error of at most 0.015.
Values may be sent and summed in bfloat16 or wider, within the bound.
A program may use at most 128 MiB of HBM per device.

v0:
```python
import jax
import jax.numpy as jnp
from jax import lax
from jax.experimental import pallas as pl
from jax.experimental.pallas import tpu as pltpu
from jax.sharding import PartitionSpec as P

HEADS = 12
HEAD_DIM = 64
WIDEN = 5

MESH = pl.DeviceIdType.MESH
F32 = jnp.float32
BF16 = jnp.bfloat16
ROOT_HALF = 0.7071067811865476
DENSITY = 0.3989422804014327


def mm(a, b):
    return jnp.dot(a, b, preferred_element_type=F32)


def mm_t(a, b):
    return lax.dot_general(a, b, (((1,), (1,)), ((), ())), preferred_element_type=F32)


def mm_tl(a, b):
    return lax.dot_general(a, b, (((0,), (0,)), ((), ())), preferred_element_type=F32)


def fold(v):
    return jnp.sum(v.reshape(v.shape[0] // 8, 8, v.shape[1]), 0)


def loop(count, body, unroll=1):
    def step(i, carry):
        body(i)
        return carry

    lax.fori_loop(0, count, step, 0, unroll=unroll)


def span_loop(first, last, body, unroll=1):
    def step(i, carry):
        body(i)
        return carry

    lax.fori_loop(first, last, step, 0, unroll=unroll)


def aligned(i, size):
    return pl.ds(pl.multiple_of(i * size, size), size)


def places():
    b, s = lax.axis_index("batch"), lax.axis_index("seq")
    x, zlo, zhi = lax.rem(b, 2), lax.rem(b // 2, 2), b // 4
    core, y = lax.rem(s, 2), s // 2
    spot = {CORE: core, X: x, Y: y, ZLO: zlo, ZHI: zhi}
    peer = {
        CORE: (b, s + 1 - 2 * core),
        Y: (b, s + 2 - 4 * y),
        X: (b + 1 - 2 * x, s),
        ZLO: (b + 2 - 4 * zlo, s),
        ZHI: (b + 4 - 8 * zhi, s),
        FAR: (b, 3 - s),
    }
    return spot, peer


class Unit:
    def __init__(self, order, both, inbox, sends, recvs, spot, peer):
        self.order, self.both, self.inbox = order, both, inbox
        self.sends, self.recvs, self.spot, self.peer = sends, recvs, spot, peer
        self.own = both.at[spot[CORE]]
        self.phase = 0

    def where(self, phase, stays):
        done, axis = self.order[: phase - 1], self.order[phase - 1]
        place = []
        for name in (Y, ZHI, ZLO, X):
            side = self.spot[name]
            if name == axis:
                place.append(side if stays else 1 - side)
            else:
                place.append(side if name in done else slice(None))
        return tuple(place)

    def copy(self, phase):
        if phase == 0:
            axis, source = CORE, self.both.at[1 - self.spot[CORE]]
        else:
            axis, source = self.order[phase - 1], self.own.at[self.where(phase, False)]
        return pltpu.make_async_remote_copy(
            src_ref=source,
            dst_ref=self.inbox[phase],
            send_sem=self.sends.at[phase],
            recv_sem=self.recvs.at[phase],
            device_id=self.peer[axis],
            device_id_type=MESH,
        )

    def start(self):
        self.copy(0).start()

    def step(self):
        phase = self.phase
        self.copy(phase).wait()
        came = self.inbox[phase]
        target = self.own if phase == 0 else self.own.at[self.where(phase, True)]
        lead = 4 - phase

        def body(n):
            place = tuple(lax.rem(n // 2 ** (lead - 1 - i), 2) for i in range(lead))
            target[place] = target[place] + came[place]

        loop(2**lead, body, 4 if phase == 0 else 1)
        self.phase = phase + 1
        self.copy(self.phase).start()


CORE, X, Y, ZLO, ZHI, FAR = range(6)
OUTER0, OUTER1, OUTER2, OUTER3, INNER0, INNER1, INNER2, INNER3, OUTPUT, QUERY, KEY, VALUE = range(0, 12)
(
    D_HIDDEN0, D_HIDDEN1, D_HIDDEN2, INNER, D_FIRST, FNB, V1, DWO,
    REFILL, DMIXED, DWQ, DWK, DWV, VEC, AB00, AB01,
    AB10, AB11, AB20, AB21, DIN0, DIN1, DIN2,
) = range(12, 35)
W1, W2, DC0, DC1, DC2, DY0, DY1, DY2 = range(35, 43)
STARTS = (
    OUTER0, OUTER1, OUTER2, OUTER3, INNER0, INNER1,
    INNER2, INNER3, OUTPUT, KEY, QUERY, VALUE,
)
ORDERS = {
    OUTER0: (Y, ZLO, X, ZHI),
    OUTER1: (X, Y, ZLO, ZHI),
    OUTER2: (Y, X, ZLO, ZHI),
    OUTER3: (ZLO, ZHI, Y, X),
    INNER0: (X, ZLO, Y, ZHI),
    INNER1: (Y, ZLO, ZHI, X),
    INNER2: (X, ZLO, Y, ZHI),
    INNER3: (Y, X, ZLO, ZHI),
    OUTPUT: (X, Y, ZLO, ZHI),
    KEY: (X, ZLO, ZHI, Y),
    QUERY: (Y, X, ZLO, ZHI),
    VALUE: (X, ZLO, Y, ZHI),
}
PLAN = (
    D_HIDDEN0, D_HIDDEN1, OUTER0, D_HIDDEN2, OUTER1, OUTER2, INNER, OUTER3,
    D_FIRST, REFILL, OUTER0, INNER0, FNB, INNER1, OUTER1, INNER2,
    V1, DWO, INNER3, W1, DMIXED, OUTER2, OUTER3, AB00,
    OUTPUT, OUTER0, INNER0, AB01, INNER1, AB10, AB11, INNER2,
    OUTER1, W1, OUTER3, INNER0, AB20, OUTER2, AB21, INNER1,
    INNER3, W1, DWK, INNER2, OUTER3, DWQ, INNER0, OUTER1,
    OUTPUT, DWV, KEY, OUTER0, INNER2, QUERY, INNER1, OUTER2,
    DIN0, INNER3, INNER0, W1, OUTER3, OUTPUT, DIN1, VALUE,
    OUTER0, OUTER1, OUTER3, INNER2, DC0, DIN2, OUTER0, OUTER2,
    INNER1, INNER3, OUTER1, DC1, QUERY, KEY, VEC, OUTER2,
    W1, OUTPUT, DC2, W2, DY0, INNER3, VALUE, KEY,
    DY1, OUTPUT, QUERY, W2, OUTPUT, VALUE, DY2, W2,
    KEY, VALUE, QUERY, W2, KEY, KEY, VALUE, QUERY,
    VALUE, W2, QUERY,
)
SLOTS = 6
ROOMS = (0, 2, 1)


def layer_body(
    hidden,
    cotangent,
    query_weight,
    key_weight,
    value_weight,
    output_weight,
    inner_weight,
    outer_weight,
    span,
    mask_embedding,
    query_bias,
    value_bias,
    output_bias,
    mixing_gain,
    mixing_shift,
    inner_bias,
    outer_bias,
    final_gain,
    final_shift,
    lengths,
    repeats,
    layer_out,
    grad_input,
    probs_out,
    out_query,
    out_key,
    out_value,
    out_output,
    out_inner,
    out_outer,
    out_vectors,
    wi,
    wf,
    wq,
    wk,
    wv,
    wo,
    packed,
    params,
    x_all,
    k_all,
    v_all,
    q_own,
    mixed,
    region,
    first_low,
    norm_one,
    spread_one,
    total,
    d_res,
    d_outer,
    d_att,
    masks,
    wide,
    inner_sums,
    mask_sums,
    grads,
    in0,
    in1,
    in2,
    in3,
    in4,
    in5,
    d_in0,
    d_in1,
    vec,
    vec_came,
    late,
    late_came,
    sends,
    recvs,
    x_send,
    x_recv,
    m_send,
    m_recv,
    v_send,
    v_recv,
    local,
    credit,
):
    spot, peer = places()
    core, y = spot[CORE], spot[Y]
    me = 2 * y + core
    sibling = 2 * y + 1 - core
    across = 2 * (1 - y) + core

    names = (CORE, X, Y, ZLO, ZHI, FAR)
    barrier = pltpu.get_barrier_semaphore()
    for name in names:
        pl.semaphore_signal(barrier, inc=1, device_id=peer[name], device_id_type=MESH)

    weight_loads = {}

    def load(name, number, source, target):
        copy = pltpu.make_async_copy(source, target, local.at[number])
        copy.start()
        weight_loads[name] = copy

    load("hidden", 0, hidden, x_all.at[:, aligned(me, 128)])
    load("key", 1, key_weight, wk)
    load("value", 2, value_weight, wv)
    load("query", 3, query_weight, wq)

    pl.semaphore_wait(barrier, len(names))

    masks[me] = jnp.zeros((8, 128), jnp.int32)
    masks[me, 0:3] = span[...]
    mask_copies = []
    for i, name in enumerate((CORE, Y, FAR)):
        copy = pltpu.make_async_remote_copy(
            src_ref=masks.at[me],
            dst_ref=masks.at[me],
            send_sem=m_send.at[i],
            recv_sem=m_recv.at[i],
            device_id=peer[name],
            device_id_type=MESH,
        )
        copy.start()
        mask_copies.append(copy)

    def x_copy(kind, r):
        source = hidden.at[r] if kind < 2 else x_all.at[r, aligned(across, 128)]
        slot = me if kind < 2 else across
        return pltpu.make_async_remote_copy(
            src_ref=source,
            dst_ref=x_all.at[r, aligned(slot, 128)],
            send_sem=x_send.at[kind, r],
            recv_sem=x_recv.at[kind, r],
            device_id=peer[Y if kind == 0 else CORE],
            device_id_type=MESH,
        )

    for r in range(3):
        x_copy(0, r).start()
        x_copy(1, r).start()

    vectors = (
        (mask_embedding, 0),
        (query_bias, 1),
        (value_bias, 2),
        (output_bias, 3),
        (mixing_gain, 4),
        (mixing_shift, 5),
        (inner_bias, 6),
        (outer_bias, 10),
        (final_gain, 11),
        (final_shift, 12),
    )
    vector_loads = []
    for i, (vector, place) in enumerate(vectors):
        target = packed.at[pl.ds(768 * place, vector.shape[0])]
        copy = pltpu.make_async_copy(vector, target, local.at[21 + i])
        copy.start()
        vector_loads.append(copy)
    for copy in vector_loads:
        copy.wait()
    for i in range(13):
        params[i : i + 1] = packed[pl.ds(768 * i, 768)].astype(F32).reshape(1, 768)

    for copy in mask_copies:
        copy.wait()
    span_all = jnp.concatenate([masks[s].astype(F32) for s in range(4)], axis=1)
    lane = lax.broadcasted_iota(jnp.int32, span_all.shape, 1)
    window = span_all
    for d in range(1, WIDEN + 1):
        window = jnp.maximum(window, jnp.where(lane >= d, pltpu.roll(span_all, d, 1), 0.0))
        window = jnp.maximum(
            window, jnp.where(lane < 512 - d, pltpu.roll(span_all, 512 - d, 1), 0.0)
        )
    wide[...] = window.T

    half = lax.broadcasted_iota(jnp.int32, (128, 128), 1) < HEAD_DIM
    zero = jnp.zeros((128, 128), BF16)

    def stacked(pair):
        return jnp.concatenate([jnp.where(half, pair, zero), jnp.where(half, zero, pair)], 0)

    def unstacked(both):
        return jnp.where(half, both[:128], both[128:])

    mask_row = params[0:1]
    spills = []

    def put_mask(r, slot):
        rows = aligned(slot, 128)
        chosen = wide[rows, r : r + 1] > 0.5
        kept = x_all[r, rows].astype(F32)
        x_all[r, rows] = jnp.where(chosen, mask_row, kept).astype(BF16)

    def project(pieces, with_queries):
        inputs = jnp.concatenate([x_all[r, aligned(slot, 128)] for r, slot in pieces], 0)

        def part(n):
            cols = aligned(n, 256)
            keys = mm(inputs, wk[:, cols]).astype(BF16)
            values = (mm(inputs, wv[:, cols]) + params[2:3, cols]).astype(BF16)
            for i, (r, slot) in enumerate(pieces):
                k_all[r, aligned(slot, 128), cols] = keys[128 * i : 128 * i + 128]
                v_all[r, aligned(slot, 128), cols] = values[128 * i : 128 * i + 128]
            if with_queries:
                q_own[:, cols] = (mm(inputs, wq[:, cols]) + params[1:2, cols]).astype(BF16)

        loop(3, part)

    weight_loads["hidden"].wait()
    for r in range(3):
        put_mask(r, me)
    for name in ("key", "value", "query"):
        weight_loads[name].wait()
    load("output", 4, output_weight, wo)
    for j in range(4):
        load(j, 5 + j, inner_weight.at[:, pl.ds(768 * j, 768)], wi.at[pl.ds(768 * j, 768)])
    load("outer", 9, outer_weight, wf)
    load("cotangent", 10, cotangent, d_outer)
    project([(r, me) for r in range(3)], True)
    for r in range(3):
        x_copy(1, r).wait()
        put_mask(r, sibling)
    project([(r, sibling) for r in range(3)], False)
    x_copy(0, 0).wait_recv()
    x_copy(2, 0).start()
    for r in range(3):
        x_copy(2, r).wait()
        put_mask(r, across)
        put_mask(r, 3 - me)
        project([(r, across), (r, 3 - me)], False)
        key_live = lax.broadcasted_iota(jnp.int32, (1, 512), 1) < lengths[r]

        def attend(p):
            cols = aligned(p, 128)
            queries = stacked(q_own[pl.ds(128 * r, 128), cols] * BF16(HEAD_DIM**-0.5))
            logits = mm_t(queries, k_all[r, :, cols])
            logits = jnp.where(key_live, logits, -1e30)
            expd = jnp.exp(logits - jnp.max(logits, -1, keepdims=True))
            probs = (expd * (1.0 / jnp.sum(expd, -1, keepdims=True))).astype(BF16)
            base = ROOMS[r] * 6 + p
            region[aligned(2 * base, 256)] = probs[:, :256]
            region[aligned(2 * base + 1, 256)] = probs[:, 256:]
            out = mm(probs, v_all[r, :, cols])
            mixed[pl.ds(128 * r, 128), cols] = unstacked(out).astype(BF16)

        def attend_three(i):
            for p in range(3):
                attend(3 * i + p)
            if r < 2:

                @pl.when(i == 0)
                def _():
                    x_copy(0, r + 1).wait_recv()
                    x_copy(2, r + 1).start()

        loop(2, attend_three)
        rows = pl.ds(3072 * ROOMS[r], 3072)
        spill = pltpu.make_async_copy(region.at[rows], probs_out.at[rows], local.at[11 + r])
        spill.start()
        spills.append(spill)

    for r in range(3):
        x_copy(0, r).wait_send()
    weight_loads["output"].wait()

    def first_norm(i):
        rows = aligned(i, 128)
        attended = mm(mixed[rows], wo[...]) + params[3:4]
        value = x_all[i, aligned(me, 128)].astype(F32) + attended
        center = value - jnp.mean(value, -1, keepdims=True)
        scale = lax.rsqrt(jnp.mean(center * center, -1, keepdims=True) + 1e-5)
        norm = center * scale
        norm_one[rows] = norm
        spread_one[rows] = scale
        first_low[rows] = (norm * params[4:5] + params[5:6]).astype(BF16)

    loop(3, first_norm)
    spills[0].wait()
    spills[1].wait()
    for j in range(4):
        weight_loads[j].wait()

    def hidden_units(j):
        inner = mm(
            first_low[...], wi[pl.ds((j // 3) * 768, 768), aligned(lax.rem(j, 3), 256)]
        ) + params[pl.ds(6 + j // 3, 1), aligned(lax.rem(j, 3), 256)]
        below = 0.5 * (1.0 + lax.erf(inner * ROOT_HALF))
        slope = below + inner * (DENSITY * jnp.exp(-0.5 * inner * inner))
        region[aligned(j, 384)] = (inner * below).astype(BF16)
        region[aligned(23 - j, 384)] = slope.astype(BF16)

    span_loop(0, 8, hidden_units, 2)
    spills[2].wait()
    span_loop(8, 12, hidden_units, 2)
    weight_loads["outer"].wait()
    weight_loads["cotangent"].wait()

    def panels(which):
        return jnp.concatenate([region[pl.ds(384 * j, 384)] for j in which], axis=1)

    def project_out(n):
        cols = aligned(n, 256)
        total[:, cols] = mm(panels(range(12)), wf[:, cols])

    loop(3, project_out, 3)

    def last_norm(i, sums):
        rows = aligned(i, 64)
        first = norm_one[rows] * params[4:5] + params[5:6]
        value = first + (total[rows] + params[10:11])
        center = value - jnp.mean(value, -1, keepdims=True)
        scale = lax.rsqrt(jnp.mean(center * center, -1, keepdims=True) + 1e-5)
        norm = center * scale
        d_att[rows] = (norm * params[11:12] + params[12:13]).astype(BF16)
        r = i // 2
        position = lax.broadcasted_iota(jnp.int32, (64, 1), 0) + lax.rem(i, 2) * 64 + me * 128
        weight = jnp.where(position < lengths[r], repeats[r].astype(F32), 0.0)
        d_final = d_outer[rows].astype(F32) * weight
        d_norm = d_final * params[11:12]
        d_two = scale * (
            d_norm
            - jnp.mean(d_norm, -1, keepdims=True)
            - norm * jnp.mean(d_norm * norm, -1, keepdims=True)
        )
        d_res[rows] = d_two
        low = d_two.astype(BF16)
        d_outer[rows] = low
        return (
            sums[0] + fold(d_final * norm),
            sums[1] + fold(d_final),
            sums[2] + fold(low.astype(F32)),
        )

    nothing = jnp.zeros((8, 768), F32)

    def put_sum(row, value):
        vec[0, row : row + 1] = jnp.sum(value, 0, keepdims=True)

    vec[0] = jnp.zeros((16, 768), F32)
    sums = lax.fori_loop(0, 6, last_norm, (nothing, nothing, nothing))
    put_sum(11, sums[0])
    put_sum(12, sums[1])
    put_sum(10, sums[2])
    out_copy = pltpu.make_async_copy(
        d_att, layer_out, local.at[14]
    )
    out_copy.start()

    units = [None] * 12
    for turn, u in enumerate(STARTS):
        inbox = [in0.at[turn % SLOTS], in1.at[u], in2.at[u], in3.at[u], in4.at[u]]
        units[u] = Unit(ORDERS[u], grads.at[u], inbox, sends.at[u], recvs.at[u], spot, peer)

    def start_unit(name):
        if STARTS.index(name) >= SLOTS:
            claim_slot()
        units[name].start()

    def free_slot():
        pl.semaphore_signal(credit, inc=1, device_id=peer[CORE], device_id_type=MESH)

    def claim_slot():
        pl.semaphore_wait(credit, 1)

    def outer_grads(z):
        for x in range(2):
            cols = [region[pl.ds(pl.multiple_of((3 * z + j) * 384, 384), 384)] for j in range(3)]
            part = jnp.concatenate(cols, axis=1)[:, 384 * x : 384 * x + 384]
            grad = mm_tl(part, d_outer[...]).astype(BF16)
            for h in range(2):
                for i in range(4):
                    for side in range(2):
                        rows = (h * 4 + i) * 48
                        grads[OUTER0 + i, h, side, z // 2, lax.rem(z, 2), x] = grad[
                            rows : rows + 48, side * 384 : side * 384 + 384
                        ]

    loop(4, outer_grads)
    for i in range(4):
        start_unit(OUTER0 + i)

    def d_hidden_units(j):
        d_act = mm_t(d_outer[...], wf[aligned(j, 256)])
        place = aligned(23 - j, 384)
        low = (d_act * region[place].astype(F32)).astype(BF16)
        region[place] = low
        inner_sums[j] = fold(low.astype(F32))

    def inner_grads(s):
        cols = [region[pl.ds(pl.multiple_of((23 - 3 * s - j) * 384, 384), 384)] for j in range(3)]
        grad = mm_tl(first_low[...], jnp.concatenate(cols, axis=1)).astype(BF16)
        for b in range(8):
            for i in range(4):
                rows, side = 96 * b + 48 * (i % 2), 384 * (i // 2)
                grads[
                    INNER0 + i, lax.rem(s, 2), s // 2, b // 4, (b // 2) % 2, b % 2
                ] = grad[rows : rows + 48, side : side + 384]

    def do_inner_grads():
        loop(4, inner_grads)
        for i in range(4):
            start_unit(INNER0 + i)

    def d_first_part(n):
        cols = aligned(n, 256)
        acc = None
        for s in range(4):
            d_inner = panels(range(23 - 3 * s, 20 - 3 * s, -1))
            term = mm_t(d_inner, wi[pl.ds(pl.multiple_of(s * 768 + n * 256, 256), 256)])
            acc = term if acc is None else acc + term
        total[:, cols] = acc

    refills = []

    def do_d_first():
        loop(3, d_first_part)
        for j in range(12):
            vec[0, 6 + j // 3 : 7 + j // 3, (j % 3) * 256 : (j % 3) * 256 + 256] = jnp.sum(
                inner_sums[j], 0, keepdims=True
            )

    def refill_probs():
        for r in range(3):
            rows = pl.ds(3072 * ROOMS[r], 3072)
            refill = pltpu.make_async_copy(probs_out.at[rows], region.at[rows], local.at[15 + r])
            refill.start()
            refills.append(refill)

    def first_norm_back(i, sums):
        rows = aligned(i, 64)
        d_first = total[rows] + d_res[rows]
        norm = norm_one[rows]
        d_norm = d_first * params[4:5]
        d_one = spread_one[rows] * (
            d_norm
            - jnp.mean(d_norm, -1, keepdims=True)
            - norm * jnp.mean(d_norm * norm, -1, keepdims=True)
        )
        d_res[rows] = d_one
        low = d_one.astype(BF16)
        d_att[rows] = low
        return (
            sums[0] + fold(d_first * norm),
            sums[1] + fold(d_first),
            sums[2] + fold(low.astype(F32)),
        )

    def do_first_norm_back():
        out_copy.wait()
        sums = lax.fori_loop(0, 6, first_norm_back, (nothing, nothing, nothing))
        put_sum(4, sums[0])
        put_sum(5, sums[1])
        put_sum(3, sums[2])

    def square_grads(u, left, right):
        for m in range(2):
            grad = mm_tl(left(m), right).astype(BF16)
            for b in range(4):
                for h in range(2):
                    for side in range(2):
                        rows = b * 96 + h * 48
                        grads[u, h, side, m, b // 2, b % 2] = grad[
                            rows : rows + 48, side * 384 : side * 384 + 384
                        ]
        start_unit(u)

    def do_output_grads():
        square_grads(OUTPUT, lambda m: mixed[:, 384 * m : 384 * m + 384], d_att[...])

    def d_mixed_part(i):
        rows = aligned(i, 128)
        mixed[rows] = mm_t(d_att[rows], wo[...]).astype(BF16)

    def do_attend_back(r, first, last):
        if first == 0:
            refills[r].wait()

        def attend_back(p):
            cols = aligned(p, 128)
            own_rows = pl.ds(128 * r, 128)
            base = ROOMS[r] * 6 + p
            queries = stacked(q_own[own_rows, cols] * BF16(HEAD_DIM**-0.5))
            d_mix = stacked(mixed[own_rows, cols])
            low_probs = jnp.concatenate(
                [region[aligned(2 * base, 256)], region[aligned(2 * base + 1, 256)]], axis=1
            )
            d_probs = mm_t(d_mix, v_all[r, :, cols])
            probs = low_probs.astype(F32)
            weighted = probs * d_probs
            d_raw = (weighted - probs * jnp.sum(weighted, -1, keepdims=True)).astype(BF16)
            d_query = mm(d_raw, k_all[r, :, cols]) * HEAD_DIM**-0.5
            q_own[own_rows, cols] = unstacked(d_query).astype(BF16)
            wi[pl.ds(512 * r, 512), cols] = mm_tl(d_raw, queries).astype(BF16)
            wi[pl.ds(1536 + 512 * r, 512), cols] = mm_tl(low_probs, d_mix).astype(BF16)

        span_loop(first, last, attend_back)

    def own_inputs(m):
        return jnp.concatenate(
            [x_all[r, aligned(me, 128), pl.ds(384 * m, 384)] for r in range(3)], 0
        )

    def all_inputs(m):
        return jnp.concatenate([x_all[r, :, pl.ds(384 * m, 384)] for r in range(3)], 0)

    def do_query_grads():
        square_grads(QUERY, own_inputs, q_own[...])

    def do_key_grads():
        square_grads(KEY, all_inputs, wi[pl.ds(0, 1536)])

    def do_value_grads():
        square_grads(VALUE, all_inputs, wi[pl.ds(1536, 1536)])

    def value_sum(i, acc):
        return acc + fold(wi[pl.ds(pl.multiple_of(1536 + i * 128, 128), 128)].astype(F32))

    mask_sums[...] = jnp.zeros((3, 8, 256), F32)

    def d_in_copy(kind, r):
        if kind == 0:
            source = wf.at[aligned(2 * r + 1 - core, 256)]
            target, name = d_in0.at[r], CORE
        else:
            source = wf.at[aligned(4 * r + 2 * core + 1 - y, 128)]
            target, name = d_in1.at[r], Y
        return pltpu.make_async_remote_copy(
            src_ref=source,
            dst_ref=target,
            send_sem=x_send.at[3 + kind, r],
            recv_sem=x_recv.at[3 + kind, r],
            device_id=peer[name],
            device_id_type=MESH,
        )

    def do_d_in(r):
        def d_in_part(n):
            cols = aligned(n, 256)
            part = mm_t(wi[pl.ds(512 * r, 512)], wk[cols]) + mm_t(
                wi[pl.ds(1536 + 512 * r, 512)], wv[cols]
            )
            for s in range(4):
                block = 4 * r + 2 * (s % 2) + s // 2
                wf[pl.ds(128 * block, 128), cols] = part[128 * s : 128 * s + 128].astype(BF16)
            mask_sums[n] = mask_sums[n] + fold(part * wide[:, r : r + 1])

        loop(3, d_in_part)
        d_in_copy(0, r).start()

    def d_in_pass(r):
        d_in_copy(0, r).wait()
        rows = aligned(4 * r + 2 * core + 1 - y, 128)
        wf[rows] = wf[rows] + d_in0[r, aligned(1 - y, 128)]
        d_in_copy(1, r).start()

    def own_part(i, acc):
        rows = aligned(i, 128)
        part = d_res[rows] + mm_t(q_own[rows], wq[...])
        d_res[rows] = part
        chosen = wide[aligned(me, 128)]
        chosen = jnp.where(i == 0, chosen[:, 0:1], jnp.where(i == 1, chosen[:, 1:2], chosen[:, 2:3]))
        return acc + fold(part * chosen)

    grad_copies = []

    def d_in_close(r):
        d_in_copy(1, r).wait()
        rows = pl.ds(128 * r, 128)
        value = (
            d_res[rows]
            + wf[aligned(4 * r + 2 * core + y, 128)].astype(F32)
            + d_in0[r, aligned(y, 128)].astype(F32)
            + d_in1[r].astype(F32)
        )
        chosen = wide[aligned(me, 128), r : r + 1] > 0.5
        d_att[rows] = jnp.where(chosen, 0.0, value).astype(BF16)
        copy = pltpu.make_async_copy(d_att.at[rows], grad_input.at[rows], local.at[18 + r])
        copy.start()
        grad_copies.append(copy)

    axes = (CORE, X, Y, ZLO, ZHI)

    def vector_copy(group, phase):
        sums, came = (vec, vec_came) if group == 0 else (late, late_came)
        return pltpu.make_async_remote_copy(
            src_ref=sums.at[phase],
            dst_ref=came.at[phase],
            send_sem=v_send.at[group, phase],
            recv_sem=v_recv.at[group, phase],
            device_id=peer[axes[phase]],
            device_id_type=MESH,
        )

    def vector_step(group, phase):
        vector_copy(group, phase).wait()
        sums, came = (vec, vec_came) if group == 0 else (late, late_came)
        sums[phase + 1] = sums[phase] + came[phase]
        if phase < 4:
            vector_copy(group, phase + 1).start()

    def do_late_sums():
        late[0] = jnp.zeros((8, 768), F32)
        mask_sum = jnp.concatenate([mask_sums[n] for n in range(3)], axis=1)
        all_sums = (
            lax.fori_loop(0, 3, own_part, mask_sum),
            fold(q_own[...].astype(F32)),
            lax.fori_loop(0, 12, value_sum, nothing),
        )
        for i, value in enumerate(all_sums):
            late[0, i : i + 1] = jnp.sum(value, 0, keepdims=True)
        vector_copy(1, 0).start()

    mine = (y, spot[ZHI], spot[ZLO], spot[X])

    def swap_copy(u):
        return pltpu.make_async_remote_copy(
            src_ref=units[u].own.at[mine],
            dst_ref=in5.at[u],
            send_sem=sends.at[u, 5],
            recv_sem=recvs.at[u, 5],
            device_id=peer[CORE],
            device_id_type=MESH,
        )

    def close(u):
        unit = units[u]
        unit.copy(4).wait()
        result = unit.own[mine].astype(F32) + unit.inbox[4][...].astype(F32)
        if INNER0 <= u < OUTPUT:
            i = u - INNER0
            out_inner[pl.ds(48 * (i % 2), 48), pl.ds(384 * (i // 2), 384)] = result
            return
        unit.own[mine] = result.astype(BF16)
        swap_copy(u).start()
        put_half(u, core, result)

    def put_half(u, side, value):
        value = jnp.where(core == 0, value[:, :192], pltpu.roll(value, 192, 1)[:, :192])
        if u < INNER0:
            out_outer[pl.ds(pl.multiple_of(side * 192 + u * 48, 48), 48)] = value
        else:
            target = (out_output, out_query, out_key, out_value)[u - OUTPUT]
            target[pl.ds(pl.multiple_of(side * 48, 48), 48)] = value

    def open_half(u):
        swap_copy(u).wait()
        put_half(u, 1 - core, in5[u].astype(F32))

    stages = {
        INNER: do_inner_grads,
        D_FIRST: do_d_first,
        FNB: do_first_norm_back,
        V1: lambda: vector_copy(0, 0).start(),
        DWO: do_output_grads,
        REFILL: refill_probs,
        DMIXED: lambda: loop(3, d_mixed_part),
        DWQ: do_query_grads,
        DWK: do_key_grads,
        DWV: do_value_grads,
        VEC: do_late_sums,
    }
    for r in range(3):
        stages[AB00 + 2 * r] = lambda r=r: do_attend_back(r, 0, 3)
        stages[AB01 + 2 * r] = lambda r=r: do_attend_back(r, 3, 6)
        stages[D_HIDDEN0 + r] = lambda r=r: span_loop(4 * r, 4 * r + 4, d_hidden_units)
        stages[DIN0 + r] = lambda r=r: do_d_in(r)
    count = {}
    for name in PLAN:
        if name in stages:
            stages[name]()
            continue
        turn = count[name] = count.get(name, -1) + 1
        if name <= VALUE:
            if turn < 4:
                units[name].step()
                if turn == 0 and STARTS.index(name) < SLOTS:
                    free_slot()
            elif turn == 4:
                close(name)
            else:
                open_half(name)
        elif name in (W1, W2):
            vector_step(name - W1, turn)
        elif name < DY0:
            d_in_pass(name - DC0)
        else:
            d_in_close(name - DY0)
    out_vectors[...] = vec[5]
    out_vectors[0:3] = late[5, 0:3]
    for copy in grad_copies:
        copy.wait()


def hand_out(*refs):
    sources, vectors, targets, rows = refs[:8], refs[8], refs[9:17], refs[17:27]
    for source, target in zip(sources[:7], targets[:7]):
        target[...] = source[...]
    targets[7][...] = sources[7][...].T
    for i, place in enumerate((0, 1, 2, 3, 4, 5, None, 10, 11, 12)):
        if place is not None:
            rows[i][...] = vectors[place]
    for j in range(4):
        rows[6][pl.ds(768 * j, 768)] = vectors[6 + j]


def fused_layer(
    hidden_in,
    cotangent,
    span_mask,
    lengths,
    repeats,
    mask_embedding,
    query_weight,
    query_bias,
    key_weight,
    value_weight,
    value_bias,
    output_weight,
    output_bias,
    mixing_gain,
    mixing_shift,
    inner_weight,
    inner_bias,
    outer_weight,
    outer_bias,
    final_gain,
    final_shift,
):
    vmem = pl.BlockSpec(memory_space=pltpu.VMEM)
    anywhere = pl.BlockSpec(memory_space=pl.ANY)
    scalars = pl.BlockSpec(memory_space=pltpu.SMEM)
    bf = lambda *shape: pltpu.VMEM(shape, BF16)
    fl = lambda *shape: pltpu.VMEM(shape, F32)
    dma = lambda *shape: pltpu.SemaphoreType.DMA(shape)
    shape = lambda dims, dtype: jax.ShapeDtypeStruct(dims, dtype)
    result = pl.pallas_call(
        layer_body,
        out_shape=[
            shape((384, 768), BF16),
            shape((384, 768), BF16),
            shape((9216, 256), BF16),
            shape((96, 192), F32),
            shape((96, 192), F32),
            shape((96, 192), F32),
            shape((96, 192), F32),
            shape((96, 768), F32),
            shape((384, 192), F32),
            shape((16, 768), F32),
        ],
        in_specs=[anywhere] * 8 + [vmem] + [anywhere] * 10 + [scalars, scalars],
        out_specs=[anywhere] * 3 + [vmem] * 7,
        scratch_shapes=[
            bf(3072, 768),
            bf(3072, 768),
            bf(768, 768),
            bf(768, 768),
            bf(768, 768),
            bf(768, 768),
            bf(13 * 768),
            fl(16, 768),
            bf(3, 512, 768),
            bf(3, 512, 768),
            bf(3, 512, 768),
            bf(384, 768),
            bf(384, 768),
            bf(9216, 256),
            bf(384, 768),
            fl(384, 768),
            fl(384, 1),
            fl(384, 768),
            fl(384, 768),
            bf(384, 768),
            bf(384, 768),
            pltpu.VMEM((4, 8, 128), jnp.int32),
            fl(512, 8),
            fl(12, 8, 256),
            fl(3, 8, 256),
            bf(12, 2, 2, 2, 2, 2, 48, 384),
            bf(SLOTS, 2, 2, 2, 2, 48, 384),
            bf(12, 2, 2, 2, 48, 384),
            bf(12, 2, 2, 48, 384),
            bf(12, 2, 48, 384),
            bf(12, 48, 384),
            bf(12, 48, 384),
            bf(3, 256, 768),
            bf(3, 128, 768),
            fl(6, 16, 768),
            fl(5, 16, 768),
            fl(6, 8, 768),
            fl(5, 8, 768),
            dma(12, 6),
            dma(12, 6),
            dma(5, 3),
            dma(5, 3),
            dma(3),
            dma(3),
            dma(2, 5),
            dma(2, 5),
            dma(31),
            pltpu.SemaphoreType.REGULAR,
        ],
        compiler_params=pltpu.CompilerParams(
            collective_id=1, has_side_effects=True, vmem_limit_bytes=63 * 2**20
        ),
        name="fused_layer",
    )(
        hidden_in,
        cotangent.reshape(384, 768),
        query_weight,
        key_weight,
        value_weight,
        output_weight,
        inner_weight,
        outer_weight,
        span_mask,
        mask_embedding,
        query_bias,
        value_bias,
        output_bias,
        mixing_gain,
        mixing_shift,
        inner_bias,
        outer_bias,
        final_gain,
        final_shift,
        lengths,
        repeats,
    )
    arrays, vectors = [result[0], result[1], *result[3:9]], result[9]
    wide_row = shape((768,), F32)
    handed = pl.pallas_call(
        hand_out,
        out_shape=[shape(v.shape, v.dtype) for v in arrays[:7]]
        + [shape((192, 384), F32)]
        + [wide_row] * 6
        + [shape((3072,), F32)]
        + [wide_row] * 3,
        in_specs=[vmem] * 9,
        out_specs=[vmem] * 18,
        name="hand_out",
    )(*arrays, vectors)
    layer_out, grad_input, g_query, g_key, g_value, g_output, g_inner, g_outer = handed[:8]
    g_mask, g_q_bias, g_v_bias, g_o_bias, g_gain, g_shift, g_inner_bias, *g_last = handed[8:]
    return (
        layer_out.reshape(3, 128, 768),
        grad_input.reshape(3, 128, 768),
        g_mask,
        g_query,
        g_q_bias,
        g_key,
        g_value,
        g_v_bias,
        g_output,
        g_o_bias,
        g_gain,
        g_shift,
        g_inner,
        g_inner_bias,
        g_outer.T,
        *g_last,
    )


def with_halo(x, sides, width):
    for axis, dim in sides:
        count, length = (lax.axis_size(axis), x.shape[dim])
        up = [(i, (i + 1) % count) for i in range(count - 1)]
        down = [(j, i) for i, j in up]
        last = lax.slice_in_dim(x, length - width, length, axis=dim)
        initial = lax.slice_in_dim(x, 0, width, axis=dim)
        before = lax.ppermute(last, axis, up)
        after = lax.ppermute(initial, axis, down)
        x = jnp.concatenate([before, x, after], axis=dim)
    return x


def layer_norm(inputs, gain, shift):
    center = inputs - jnp.mean(inputs, -1, keepdims=True)
    spread = jnp.mean(center * center, -1, keepdims=True)
    return center * lax.rsqrt(spread + 1e-05) * gain + shift


def linear(inputs, weight):
    return jnp.dot(inputs, weight, preferred_element_type=jnp.float32)


def linear_back(grads, weight):
    return lax.dot_general(
        grads, weight, (((1,), (1,)), ((), ())), preferred_element_type=jnp.float32
    )


def contract_rows(left, right):
    return lax.dot_general(
        left, right, (((0,), (0,)), ((), ())), preferred_element_type=jnp.float32
    )


def gelu_exact(inputs):
    return jax.nn.gelu(inputs, approximate=False)


def plain_layer(
    hidden_in,
    cotangent,
    span_mask,
    lengths,
    repeats,
    mask_embedding,
    query_weight,
    query_bias,
    key_weight,
    value_weight,
    value_bias,
    output_weight,
    output_bias,
    mixing_gain,
    mixing_shift,
    inner_weight,
    inner_bias,
    outer_weight,
    outer_bias,
    final_gain,
    final_shift,
):
    rows, stretch, width = hidden_in.shape
    whole = stretch * lax.axis_size("seq")
    scale = HEAD_DIM ** (-0.5)
    offset = lax.axis_index("seq") * stretch
    rim = with_halo(span_mask, (("seq", 1),), WIDEN)
    window = rim[:, 0:stretch]
    for shifted in range(1, 2 * WIDEN + 1):
        window = window + rim[:, shifted : shifted + stretch]
    widened = window > 0
    positions = offset + jnp.arange(stretch, dtype=jnp.int32)
    live = positions[None, :] < lengths[:, None]
    key_live = jnp.arange(whole, dtype=jnp.int32)[None, :] < lengths[:, None]
    masked_in = jnp.where(widened[..., None], mask_embedding[None, None, :], hidden_in)
    flat_in = masked_in.reshape(rows * stretch, width)
    queries = (linear(flat_in, query_weight) + query_bias.astype(jnp.float32)).astype(jnp.bfloat16)
    key_rows = linear(flat_in, key_weight).astype(jnp.bfloat16).reshape(rows, stretch, width)
    value_rows = (linear(flat_in, value_weight) + value_bias.astype(jnp.float32)).astype(
        jnp.bfloat16
    )
    value_rows = value_rows.reshape(rows, stretch, width)
    key_all, value_all = (
        lax.all_gather(key_rows, "seq", axis=1, tiled=True),
        lax.all_gather(value_rows, "seq", axis=1, tiled=True),
    )
    query_heads = queries.reshape(rows, stretch, HEADS, HEAD_DIM)

    def scores_of(key_full):
        key_heads = key_full.reshape(rows, whole, HEADS, HEAD_DIM)
        raw = jnp.einsum(
            "rqhd,rkhd->rhqk", query_heads, key_heads, preferred_element_type=jnp.float32
        )
        return jnp.where(key_live[:, None, None, :], raw * scale, -1e30)

    logits = scores_of(key_all)
    highest = jnp.max(logits, -1, keepdims=True)
    expd = jnp.exp(logits - highest)
    totals = jnp.sum(expd, -1, keepdims=True)
    log_total = highest + jnp.log(totals)
    probs_low = (expd / totals).astype(jnp.bfloat16)
    value_heads = value_all.reshape(rows, whole, HEADS, HEAD_DIM)
    mixed = jnp.einsum(
        "rhqk,rkhd->rqhd", probs_low, value_heads, preferred_element_type=jnp.float32
    )
    mixed = mixed.reshape(rows * stretch, width).astype(jnp.bfloat16)
    attended = linear(mixed, output_weight) + output_bias.astype(jnp.float32)
    residual_one = flat_in.astype(jnp.float32) + attended
    first, norm_back_one = jax.vjp(
        layer_norm, residual_one, mixing_gain.astype(jnp.float32), mixing_shift.astype(jnp.float32)
    )
    first_low = first.astype(jnp.bfloat16)
    inner = linear(first_low, inner_weight) + inner_bias.astype(jnp.float32)
    activated, gelu_back = jax.vjp(gelu_exact, inner)
    activated_low = activated.astype(jnp.bfloat16)
    outer = linear(activated_low, outer_weight) + outer_bias.astype(jnp.float32)
    final, norm_back_two = jax.vjp(
        layer_norm, first + outer, final_gain.astype(jnp.float32), final_shift.astype(jnp.float32)
    )
    layer_out = final.astype(jnp.bfloat16).reshape(rows, stretch, width)
    weighting = repeats.astype(jnp.float32)[:, None] * live.astype(jnp.float32)
    d_final = (cotangent.astype(jnp.float32) * weighting[:, :, None]).reshape(rows * stretch, width)
    d_two, d_final_gain, d_final_shift = norm_back_two(d_final)
    d_outer = d_two.astype(jnp.bfloat16)
    g_outer_weight = contract_rows(activated_low, d_outer)
    g_outer_bias = jnp.sum(d_outer.astype(jnp.float32), 0)
    (d_inner,) = gelu_back(linear_back(d_outer, outer_weight))
    d_inner = d_inner.astype(jnp.bfloat16)
    g_inner_weight = contract_rows(first_low, d_inner)
    g_inner_bias = jnp.sum(d_inner.astype(jnp.float32), 0)
    d_first = linear_back(d_inner, inner_weight) + d_two
    d_one, d_mixing_gain, d_mixing_shift = norm_back_one(d_first)
    d_attended = d_one.astype(jnp.bfloat16)
    g_output_weight = contract_rows(mixed, d_attended)
    g_output_bias = jnp.sum(d_attended.astype(jnp.float32), 0)
    d_mixed = linear_back(d_attended, output_weight).astype(jnp.bfloat16)
    d_mixed_heads = d_mixed.reshape(rows, stretch, HEADS, HEAD_DIM)
    key_back, value_back = (
        lax.all_gather(key_rows, "seq", axis=1, tiled=True),
        lax.all_gather(value_rows, "seq", axis=1, tiled=True),
    )
    probs = jnp.exp(scores_of(key_back) - log_total)
    probs_again = probs.astype(jnp.bfloat16)
    key_heads = key_back.reshape(rows, whole, HEADS, HEAD_DIM)
    value_heads = value_back.reshape(rows, whole, HEADS, HEAD_DIM)
    d_probs = jnp.einsum(
        "rqhd,rkhd->rhqk", d_mixed_heads, value_heads, preferred_element_type=jnp.float32
    )
    centered = d_probs - jnp.sum(probs * d_probs, -1, keepdims=True)
    d_raw = (probs * centered * scale).astype(jnp.bfloat16)
    d_queries = jnp.einsum("rhqk,rkhd->rqhd", d_raw, key_heads, preferred_element_type=jnp.float32)
    d_queries = d_queries.reshape(rows * stretch, width).astype(jnp.bfloat16)
    d_key_part = jnp.einsum(
        "rhqk,rqhd->rkhd", d_raw, query_heads, preferred_element_type=jnp.float32
    )
    d_value_part = jnp.einsum(
        "rhqk,rqhd->rkhd", probs_again, d_mixed_heads, preferred_element_type=jnp.float32
    )
    d_key_sum, d_value_sum = (
        lax.psum_scatter(
            d_key_part.reshape(rows, whole, width), "seq", scatter_dimension=1, tiled=True
        ),
        lax.psum_scatter(
            d_value_part.reshape(rows, whole, width), "seq", scatter_dimension=1, tiled=True
        ),
    )
    d_keys = d_key_sum.astype(jnp.bfloat16).reshape(rows * stretch, width)
    d_values = d_value_sum.astype(jnp.bfloat16).reshape(rows * stretch, width)
    g_query_weight = contract_rows(flat_in, d_queries)
    g_key_weight = contract_rows(flat_in, d_keys)
    g_value_weight = contract_rows(flat_in, d_values)
    g_query_bias = jnp.sum(d_queries.astype(jnp.float32), 0)
    g_value_bias = jnp.sum(d_values.astype(jnp.float32), 0)
    d_input = (
        d_one
        + linear_back(d_queries, query_weight)
        + linear_back(d_keys, key_weight)
        + linear_back(d_values, value_weight)
    ).reshape(rows, stretch, width)
    grad_input = jnp.where(widened[..., None], 0.0, d_input).astype(jnp.bfloat16)
    g_mask = jnp.sum(jnp.where(widened[..., None], d_input, 0.0), (0, 1))
    matrices = (
        g_query_weight,
        g_key_weight,
        g_value_weight,
        g_output_weight,
        g_inner_weight,
        g_outer_weight,
    )
    partial_sums = (
        lax.psum_scatter(matrices[0], "batch", scatter_dimension=0, tiled=True),
        lax.psum_scatter(matrices[1], "batch", scatter_dimension=0, tiled=True),
        lax.psum_scatter(matrices[2], "batch", scatter_dimension=0, tiled=True),
        lax.psum_scatter(matrices[3], "batch", scatter_dimension=0, tiled=True),
        lax.psum_scatter(matrices[4], "batch", scatter_dimension=0, tiled=True),
        lax.psum_scatter(matrices[5], "batch", scatter_dimension=0, tiled=True),
    )
    summed = (
        lax.psum_scatter(partial_sums[0], "seq", scatter_dimension=1, tiled=True),
        lax.psum_scatter(partial_sums[1], "seq", scatter_dimension=1, tiled=True),
        lax.psum_scatter(partial_sums[2], "seq", scatter_dimension=1, tiled=True),
        lax.psum_scatter(partial_sums[3], "seq", scatter_dimension=1, tiled=True),
        lax.psum_scatter(partial_sums[4], "seq", scatter_dimension=1, tiled=True),
        lax.psum_scatter(partial_sums[5], "seq", scatter_dimension=1, tiled=True),
    )
    vectors = lax.psum(
        (
            g_mask,
            g_query_bias,
            g_value_bias,
            g_output_bias,
            d_mixing_gain,
            d_mixing_shift,
            g_inner_bias,
            g_outer_bias,
            d_final_gain,
            d_final_shift,
        ),
        ("batch", "seq"),
    )
    return (
        layer_out,
        grad_input,
        vectors[0],
        summed[0],
        vectors[1],
        summed[1],
        summed[2],
        vectors[2],
        summed[3],
        vectors[3],
        vectors[4],
        vectors[5],
        summed[4],
        vectors[6],
        summed[5],
        vectors[7],
        vectors[8],
        vectors[9],
    )


def solution(mesh):
    fused = mesh.shape["batch"] == 8 and mesh.shape["seq"] == 4
    return jax.shard_map(
        fused_layer if fused else plain_layer,
        mesh=mesh,
        in_specs=(
            P("batch", "seq", None),
            P("batch", "seq", None),
            P("batch", "seq"),
            P("batch"),
            P("batch"),
            P(),
            P(),
            P(),
            P(),
            P(),
            P(),
            P(),
            P(),
            P(),
            P(),
            P(),
            P(),
            P(),
            P(),
            P(),
            P(),
        ),
        out_specs=(
            P("batch", "seq", None),
            P("batch", "seq", None),
            P(),
            P("batch", "seq"),
            P(),
            P("batch", "seq"),
            P("batch", "seq"),
            P(),
            P("batch", "seq"),
            P(),
            P(),
            P(),
            P("batch", "seq"),
            P(),
            P("batch", "seq"),
            P(),
            P(),
            P(),
        ),
        check_vma=False,
    )
```

profile of v0, /device:TPU:0, one launch (start us, length us, event | category | flops | bytes accessed | tf_op | source)
XLA Modules:
  0.0 119.6 jit_solution(1523272741867516392)
XLA Ops:
  0.7 115.7 %fused_layer.1 = (bf16[384,768]{1,0:T(8,128)(2,1)}, bf16[384,768]{1,0:T(8,128)(2,1)}, bf16[9216,256]{1,0:T(8,128)(2,1)}, f32[96,192]{1,0:T(8,128)}, f32[96,192]{...) custom-call(bf16[3,128,768]{2,1,0:T(8,128)(2,1)} %hidden.1, ...), custom_call_target="tpu_custom_call" | custom-call | tf_op jit(solution)/shard_map/fused_layer/pallas_call | solution.py:900
  116.4 3.0 %hand_out.1 = (bf16[384,768]{1,0:T(8,128)(2,1)}, bf16[384,768]{1,0:T(8,128)(2,1)}, f32[96,192]{1,0:T(8,128)}, f32[96,192]{1,0:T(8,128)}, f32[96,192]{1,0:T(8,128...) custom-call(bf16[384,768]{1,0:T(8,128)(2,1)} %get-tuple-element.45.r, ...), custom_call_target="tpu_custom_call" | custom-call | tf_op jit(solution)/shard_map/hand_out/pallas_call | solution.py:995
where the time goes:
time: 120 us
  Pallas kernels  119 us (99%)
    pallas_call x1, Pallas kernels, fused_layer(): pl.pallas_call(layer_body, out_shape=[shape((384, 768), BF16), shape((384...  116 us
    pallas_call x1, Pallas kernels, fused_layer(): pl.pallas_call(hand_out, out_shape=[shape(v.shape, v.dtype) for v in arra...  3.04 us

commit v1 on v0

--- a/solution.py
+++ b/solution.py
@@ -114,7 +114,7 @@
             place = tuple(lax.rem(n // 2 ** (lead - 1 - i), 2) for i in range(lead))
             target[place] = target[place] + came[place]
 
-        loop(2**lead, body, 4 if phase == 0 else 1)
+        loop(2**lead, body, min(4, 2**lead))
         self.phase = phase + 1
         self.copy(self.phase).start()
 
@@ -368,7 +368,7 @@
             if with_queries:
                 q_own[:, cols] = (mm(inputs, wq[:, cols]) + params[1:2, cols]).astype(BF16)
 
-        loop(3, part)
+        loop(3, part, 3)
 
     weight_loads["hidden"].wait()
     for r in range(3):
@@ -438,7 +438,7 @@
         spread_one[rows] = scale
         first_low[rows] = (norm * params[4:5] + params[5:6]).astype(BF16)
 
-    loop(3, first_norm)
+    loop(3, first_norm, 3)
     spills[0].wait()
     spills[1].wait()
     for j in range(4):
@@ -453,7 +453,7 @@
         region[aligned(j, 384)] = (inner * below).astype(BF16)
         region[aligned(23 - j, 384)] = slope.astype(BF16)
 
-    span_loop(0, 8, hidden_units, 2)
+    span_loop(0, 8, hidden_units, 4)
     spills[2].wait()
     span_loop(8, 12, hidden_units, 2)
     weight_loads["outer"].wait()
@@ -539,7 +539,7 @@
                             rows : rows + 48, side * 384 : side * 384 + 384
                         ]
 
-    loop(4, outer_grads)
+    loop(4, outer_grads, 2)
     for i in range(4):
         start_unit(OUTER0 + i)
 
@@ -561,7 +561,7 @@
                 ] = grad[rows : rows + 48, side : side + 384]
 
     def do_inner_grads():
-        loop(4, inner_grads)
+        loop(4, inner_grads, 2)
         for i in range(4):
             start_unit(INNER0 + i)
 

time: 120 us -> 116 us (0.967)
  Pallas kernels: 119 us -> 115 us
    pallas_call x1, Pallas kernels: 116 us -> 112 us  [fused_layer(): pl.pallas_call(layer_body, out_shape=[shape((384, 768), BF16), shape((384...]
where the time goes in v1:
time: 116 us
  Pallas kernels  115 us (99%)
    pallas_call x1, Pallas kernels, fused_layer(): pl.pallas_call(layer_body, out_shape=[shape((384, 768), BF16), shape((384...  112 us
    pallas_call x1, Pallas kernels, fused_layer(): pl.pallas_call(hand_out, out_shape=[shape(v.shape, v.dtype) for v in arra...  3.04 us

profile of v1, /device:TPU:0, one launch (start us, length us, event | category | flops | bytes accessed | tf_op | source)
XLA Modules:
  0.0 116.1 jit_solution(10766634081952494506)
XLA Ops:
  0.7 112.2 %fused_layer.1 = (bf16[384,768]{1,0:T(8,128)(2,1)}, bf16[384,768]{1,0:T(8,128)(2,1)}, bf16[9216,256]{1,0:T(8,128)(2,1)}, f32[96,192]{1,0:T(8,128)}, f32[96,192]{...) custom-call(bf16[3,128,768]{2,1,0:T(8,128)(2,1)} %hidden.1, ...), custom_call_target="tpu_custom_call" | custom-call | tf_op jit(solution)/shard_map/fused_layer/pallas_call | solution.py:900
  112.8 3.0 %hand_out.1 = (bf16[384,768]{1,0:T(8,128)(2,1)}, bf16[384,768]{1,0:T(8,128)(2,1)}, f32[96,192]{1,0:T(8,128)}, f32[96,192]{1,0:T(8,128)}, f32[96,192]{1,0:T(8,128...) custom-call(bf16[384,768]{1,0:T(8,128)(2,1)} %get-tuple-element.45.r, ...), custom_call_target="tpu_custom_call" | custom-call | tf_op jit(solution)/shard_map/hand_out/pallas_call | solution.py:995

commit v2 on v1

--- a/solution.py
+++ b/solution.py
@@ -132,14 +132,14 @@
     INNER2, INNER3, OUTPUT, KEY, QUERY, VALUE,
 )
 ORDERS = {
-    OUTER0: (Y, ZLO, X, ZHI),
-    OUTER1: (X, Y, ZLO, ZHI),
-    OUTER2: (Y, X, ZLO, ZHI),
-    OUTER3: (ZLO, ZHI, Y, X),
-    INNER0: (X, ZLO, Y, ZHI),
-    INNER1: (Y, ZLO, ZHI, X),
-    INNER2: (X, ZLO, Y, ZHI),
-    INNER3: (Y, X, ZLO, ZHI),
+    OUTER0: (ZLO, Y, ZHI, X),
+    OUTER1: (Y, X, ZLO, ZHI),
+    OUTER2: (X, ZLO, Y, ZHI),
+    OUTER3: (ZLO, Y, ZHI, X),
+    INNER0: (X, Y, ZLO, ZHI),
+    INNER1: (ZLO, Y, X, ZHI),
+    INNER2: (X, Y, ZLO, ZHI),
+    INNER3: (Y, ZLO, ZHI, X),
     OUTPUT: (X, Y, ZLO, ZHI),
     KEY: (X, ZLO, ZHI, Y),
     QUERY: (Y, X, ZLO, ZHI),
@@ -147,19 +147,19 @@
 }
 PLAN = (
     D_HIDDEN0, D_HIDDEN1, OUTER0, D_HIDDEN2, OUTER1, OUTER2, INNER, OUTER3,
-    D_FIRST, REFILL, OUTER0, INNER0, FNB, INNER1, OUTER1, INNER2,
-    V1, DWO, INNER3, W1, DMIXED, OUTER2, OUTER3, AB00,
-    OUTPUT, OUTER0, INNER0, AB01, INNER1, AB10, AB11, INNER2,
-    OUTER1, W1, OUTER3, INNER0, AB20, OUTER2, AB21, INNER1,
-    INNER3, W1, DWK, INNER2, OUTER3, DWQ, INNER0, OUTER1,
-    OUTPUT, DWV, KEY, OUTER0, INNER2, QUERY, INNER1, OUTER2,
-    DIN0, INNER3, INNER0, W1, OUTER3, OUTPUT, DIN1, VALUE,
-    OUTER0, OUTER1, OUTER3, INNER2, DC0, DIN2, OUTER0, OUTER2,
-    INNER1, INNER3, OUTER1, DC1, QUERY, KEY, VEC, OUTER2,
-    W1, OUTPUT, DC2, W2, DY0, INNER3, VALUE, KEY,
-    DY1, OUTPUT, QUERY, W2, OUTPUT, VALUE, DY2, W2,
-    KEY, VALUE, QUERY, W2, KEY, KEY, VALUE, QUERY,
-    VALUE, W2, QUERY,
+    D_FIRST, REFILL, FNB, INNER0, OUTER0, INNER1, OUTER1, OUTER2,
+    INNER2, V1, DWO, INNER3, W1, DMIXED, OUTER3, OUTER0,
+    AB00, OUTPUT, AB01, INNER0, AB10, OUTER1, INNER3, INNER1,
+    AB11, OUTER2, AB20, OUTER3, AB21, INNER2, OUTER0, W1,
+    OUTER1, INNER0, DWK, INNER3, INNER1, DWQ, DWV, KEY,
+    OUTER2, OUTPUT, OUTER1, QUERY, INNER2, OUTER0, OUTER3, INNER0,
+    DIN0, OUTER0, W1, OUTER1, INNER1, DIN1, VALUE, INNER3,
+    OUTER2, INNER2, DC0, OUTPUT, DIN2, OUTER2, W1, KEY,
+    INNER0, DC1, OUTER3, VEC, INNER1, INNER2, OUTER3, QUERY,
+    DC2, OUTPUT, W2, W1, VALUE, DY0, INNER3, KEY,
+    OUTPUT, QUERY, W2, OUTPUT, DY1, VALUE, KEY, DY2,
+    W2, QUERY, VALUE, W2, KEY, KEY, QUERY, VALUE,
+    QUERY, W2, VALUE,
 )
 SLOTS = 6
 ROOMS = (0, 2, 1)

time: 116 us -> 115 us (level)
  no operation moved by 1% of the time
where the time goes in v2:
time: 115 us
  Pallas kernels  114 us (99%)
    pallas_call x1, Pallas kernels, fused_layer(): pl.pallas_call(layer_body, out_shape=[shape((384, 768), BF16), shape((384...  111 us
    pallas_call x1, Pallas kernels, fused_layer(): pl.pallas_call(hand_out, out_shape=[shape(v.shape, v.dtype) for v in arra...  3.04 us

profile of v2, /device:TPU:0, one launch (start us, length us, event | category | flops | bytes accessed | tf_op | source)
XLA Modules:
  0.0 115.2 jit_solution(17952564634399912746)
XLA Ops:
  0.7 111.3 %fused_layer.1 = (bf16[384,768]{1,0:T(8,128)(2,1)}, bf16[384,768]{1,0:T(8,128)(2,1)}, bf16[9216,256]{1,0:T(8,128)(2,1)}, f32[96,192]{1,0:T(8,128)}, f32[96,192]{...) custom-call(bf16[3,128,768]{2,1,0:T(8,128)(2,1)} %hidden.1, ...), custom_call_target="tpu_custom_call" | custom-call | tf_op jit(solution)/shard_map/fused_layer/pallas_call | solution.py:900
  112.0 3.0 %hand_out.1 = (bf16[384,768]{1,0:T(8,128)(2,1)}, bf16[384,768]{1,0:T(8,128)(2,1)}, f32[96,192]{1,0:T(8,128)}, f32[96,192]{1,0:T(8,128)}, f32[96,192]{1,0:T(8,128...) custom-call(bf16[384,768]{1,0:T(8,128)(2,1)} %get-tuple-element.45.r, ...), custom_call_target="tpu_custom_call" | custom-call | tf_op jit(solution)/shard_map/hand_out/pallas_call | solution.py:995

commit v3 on v2

--- a/solution.py
+++ b/solution.py
@@ -455,7 +455,7 @@
 
     span_loop(0, 8, hidden_units, 4)
     spills[2].wait()
-    span_loop(8, 12, hidden_units, 2)
+    span_loop(8, 12, hidden_units, 4)
     weight_loads["outer"].wait()
     weight_loads["cotangent"].wait()
 
@@ -501,7 +501,7 @@
         vec[0, row : row + 1] = jnp.sum(value, 0, keepdims=True)
 
     vec[0] = jnp.zeros((16, 768), F32)
-    sums = lax.fori_loop(0, 6, last_norm, (nothing, nothing, nothing))
+    sums = lax.fori_loop(0, 6, last_norm, (nothing, nothing, nothing), unroll=2)
     put_sum(11, sums[0])
     put_sum(12, sums[1])
     put_sum(10, sums[2])
@@ -539,7 +539,7 @@
                             rows : rows + 48, side * 384 : side * 384 + 384
                         ]
 
-    loop(4, outer_grads, 2)
+    loop(4, outer_grads, 4)
     for i in range(4):
         start_unit(OUTER0 + i)
 
@@ -577,7 +577,7 @@
     refills = []
 
     def do_d_first():
-        loop(3, d_first_part)
+        loop(3, d_first_part, 3)
         for j in range(12):
             vec[0, 6 + j // 3 : 7 + j // 3, (j % 3) * 256 : (j % 3) * 256 + 256] = jnp.sum(
                 inner_sums[j], 0, keepdims=True
@@ -611,7 +611,7 @@
 
     def do_first_norm_back():
         out_copy.wait()
-        sums = lax.fori_loop(0, 6, first_norm_back, (nothing, nothing, nothing))
+        sums = lax.fori_loop(0, 6, first_norm_back, (nothing, nothing, nothing), unroll=2)
         put_sum(4, sums[0])
         put_sum(5, sums[1])
         put_sum(3, sums[2])
@@ -826,7 +826,7 @@
     for r in range(3):
         stages[AB00 + 2 * r] = lambda r=r: do_attend_back(r, 0, 3)
         stages[AB01 + 2 * r] = lambda r=r: do_attend_back(r, 3, 6)
-        stages[D_HIDDEN0 + r] = lambda r=r: span_loop(4 * r, 4 * r + 4, d_hidden_units)
+        stages[D_HIDDEN0 + r] = lambda r=r: span_loop(4 * r, 4 * r + 4, d_hidden_units, 2)
         stages[DIN0 + r] = lambda r=r: do_d_in(r)
     count = {}
     for name in PLAN:

time: 115 us -> 115 us (level)
  no operation moved by 1% of the time
where the time goes in v3:
time: 115 us; the launch traced here: 114 us
  Pallas kernels  114 us (99%)
    pallas_call x1, Pallas kernels, fused_layer(): pl.pallas_call(layer_body, out_shape=[shape((384, 768), BF16), shape((384...  111 us
    pallas_call x1, Pallas kernels, fused_layer(): pl.pallas_call(hand_out, out_shape=[shape(v.shape, v.dtype) for v in arra...  3.04 us

profile of v3, /device:TPU:0, one launch (start us, length us, event | category | flops | bytes accessed | tf_op | source)
XLA Modules:
  0.0 114.5 jit_solution(14125798854093307747)
XLA Ops:
  0.7 110.6 %fused_layer.1 = (bf16[384,768]{1,0:T(8,128)(2,1)}, bf16[384,768]{1,0:T(8,128)(2,1)}, bf16[9216,256]{1,0:T(8,128)(2,1)}, f32[96,192]{1,0:T(8,128)}, f32[96,192]{...) custom-call(bf16[3,128,768]{2,1,0:T(8,128)(2,1)} %hidden.1, ...), custom_call_target="tpu_custom_call" | custom-call | tf_op jit(solution)/shard_map/fused_layer/pallas_call | solution.py:900
  111.2 3.0 %hand_out.1 = (bf16[384,768]{1,0:T(8,128)(2,1)}, bf16[384,768]{1,0:T(8,128)(2,1)}, f32[96,192]{1,0:T(8,128)}, f32[96,192]{1,0:T(8,128)}, f32[96,192]{1,0:T(8,128...) custom-call(bf16[384,768]{1,0:T(8,128)(2,1)} %get-tuple-element.45.r, ...), custom_call_target="tpu_custom_call" | custom-call | tf_op jit(solution)/shard_map/hand_out/pallas_call | solution.py:995
